TPU v7x, 32 devices: a whole 2x2x4 slice. The times are simulated.
32 devices in a mesh: band: 4 (over x, core), dom: 8 (over z, y).
Axes of the slice: x: 2, y: 2, z: 4, core: 2. Of those that a mesh axis runs over, the one named last changes fastest.
Arguments:
- occupied: float32 [256, 12288], P('band', 'dom'), may hold values from -6 to 6
- start_guess: float32 [1, 256, 12288], P(None, 'band', 'dom'), may hold values from -0.6 to 0.6
- potential: float32 [12288], P('dom'), may hold values from 0.5 to 8
- perturbation: float32 [1, 12288], P(None, 'dom'), may hold values from -6 to 6
- band_energy: float32 [256], P('band'), may hold values from -4 to -0.5
- beta_radial: float32 [512], replicated, may hold values from -0.25 to 0.25
- beta_slope: float32 [512], replicated, may hold values from -0.25 to 0.25
- atom_owner: int32 [32], replicated, may hold values from 0 to 7, as said below
- atom_site: int32 [3, 32], replicated, may hold values from 0 to 15, as said below
- sphere_offset: int32 [3, 512], replicated, may hold values from -5 to 5
- displaced: int32 [1], replicated, may hold values from 0 to 31
Outputs:
- solution: float32 [1, 256, 12288], P(None, 'band', 'dom')
- residual: float32 [1, 256, 12288], P(None, 'band', 'dom')
Inputs may be any that keep to these rules, and one draw needn't show every extreme that they name: `atom_owner`: each slab owns at most 8 atoms and some slab owns exactly 8. `atom_site`: row 0 lies below 6, row 1 below 16, row 2 below 16. Atom 0 sits on plane 5 of its slab, row 15 and column 15; atom 1 on plane 0, row 0 and column 0.
All inputs are finite; a program needn't handle non-finite values.
Results may differ from a plain program's by a relative error of at most 0.0003.
Values sent between devices are 32-bit elements; how exact they have to be, the bound alone decides.
A program may use at most 128 MiB of HBM per device.

v0:
```python
import functools
import numpy as np
import jax
import jax.numpy as jnp
from jax import lax
from jax.experimental import pallas as pl
from jax.experimental.pallas import tpu as pltpu
from jax.sharding import PartitionSpec as P

NY = 16
NX = 16
PLANE = NY * NX
HALO = 6
RAD = 5

COEF = (
    -5369.0 / 1800.0,
    12.0 / 7.0,
    -15.0 / 56.0,
    10.0 / 189.0,
    -1.0 / 112.0,
    2.0 / 825.0,
    -1.0 / 1386.0,
)
KINETIC = 2.0
SHIFT = 20.0
STRENGTH = 10.0
HIGH = lax.Precision.HIGHEST


def plane_matrix():
    full = np.zeros((PLANE, PLANE), np.float64)
    for y in range(NY):
        for x in range(NX):
            at = y * NX + x
            full[at, at] += 3.0 * COEF[0]
            for d in range(1, 7):
                for s in (d, -d):
                    full[((y + s) % NY) * NX + x, at] += COEF[d]
                    full[y * NX + (x + s) % NX, at] += COEF[d]
    return (-KINETIC * full).astype(np.float32)


def fields_kernel(slabs, depth, radial, slope, offset, owner, site, displaced, out, pair, padded):
    atoms = out.shape[0]
    planes = slabs * depth
    points = offset.shape[1]
    slab = lax.axis_index("dom")
    rows = lax.broadcasted_iota(jnp.int32, (16, points), 0)
    along_z = rows == offset[0:1, :] + RAD
    in_plane = (offset[1:2, :] & (NY - 1)) * NX + (offset[2:3, :] & (NX - 1))
    hot = jnp.where(
        lax.broadcasted_iota(jnp.int32, (PLANE, points), 0) == in_plane, 1.0, 0.0
    ).astype(jnp.float32)
    left = jnp.concatenate(
        [jnp.where(along_z, radial[...], 0.0), jnp.where(along_z, slope[...], 0.0)], axis=0
    )
    template = lax.dot_general(
        left, hot, (((1,), (1,)), ((), ())), precision=HIGH, preferred_element_type=jnp.float32
    )
    padded[...] = jnp.zeros_like(padded)
    for which in range(2):
        part = template[16 * which : 16 * which + 16]
        padded[which, 0:16, :] = part
        padded[which, planes : planes + 16, :] = part
    column = lax.broadcasted_iota(jnp.int32, (8, PLANE), 1) & (NX - 1)

    def shifted(which, a):
        z = lax.rem(slab * depth + RAD + 2 * planes - owner[a] * depth - site[0, a], planes)
        x = site[2, a]
        turn = site[1, a] * NX + x
        start = pl.multiple_of(lax.div(z, 8) * 8, 8)
        block = pltpu.roll(padded[which, pl.ds(start, 16), :], lax.rem(16 - lax.rem(z, 8), 16), 0)[0:8]
        first = pltpu.roll(block, turn, 1)
        second = pltpu.roll(block, lax.rem(turn + PLANE - NX, PLANE), 1)
        return jnp.where(column >= x, first, second)

    for a in range(atoms):
        field = shifted(0, a)
        for z in range(depth):
            out[a : a + 1, z * PLANE : (z + 1) * PLANE] = field[z : z + 1]
    pair[...] = jnp.zeros_like(pair)
    for which in range(2):
        field = shifted(which, displaced[0])
        for z in range(depth):
            pair[which : which + 1, z * PLANE : (z + 1) * PLANE] = field[z : z + 1]


def atom_fields(slabs, cells, beta_radial, beta_slope, offset, owner, site, displaced):
    atoms = owner.shape[0]
    depth = cells // PLANE
    vmem = pl.BlockSpec(memory_space=pltpu.VMEM)
    smem = pl.BlockSpec(memory_space=pltpu.SMEM)
    return pl.pallas_call(
        functools.partial(fields_kernel, slabs, depth),
        out_shape=(
            jax.ShapeDtypeStruct((atoms, cells), jnp.float32),
            jax.ShapeDtypeStruct((8, cells), jnp.float32),
        ),
        in_specs=[vmem, vmem, vmem, smem, smem, smem],
        out_specs=(vmem, vmem),
        scratch_shapes=[pltpu.VMEM((2, slabs * depth + 16, PLANE), jnp.float32)],
        compiler_params=pltpu.CompilerParams(vmem_limit_bytes=16 * 1024 * 1024),
    )(beta_radial[None, :], beta_slope[None, :], offset, owner, site, displaced)


def times(a, b, dims):
    return lax.dot_general(a, b, (dims, ((), ())), precision=HIGH, preferred_element_type=jnp.float32)


def plain(occupied, start, potential, perturbation, energy, beta, pair, in_plane):
    slabs = lax.axis_size("dom")
    bands, cells = start.shape
    depth = cells // PLANE
    total = cells * slabs
    whole = lax.all_gather(occupied, "band", axis=0, tiled=True)
    every = whole.shape[0]
    up = [(i, (i + 1) % slabs) for i in range(slabs)]
    down = [(j, i) for i, j in up]

    def local_part(field):
        before = lax.ppermute(field, "dom", up)
        after = lax.ppermute(field, "dom", down)
        grid = jnp.concatenate([before, field, after], axis=1)
        image = times(field.reshape(bands * depth, PLANE), in_plane, ((1,), (0,))).reshape(bands, cells)
        for d in range(1, 7):
            low = (depth - d) * PLANE
            high = (depth + d) * PLANE
            image += (-KINETIC * COEF[d]) * (grid[:, low : low + cells] + grid[:, high : high + cells])
        return image + (potential - energy) * field

    def correlate(field):
        return jnp.concatenate(
            [times(field, whole, ((1,), (1,))), times(field, beta, ((1,), (1,)))], axis=1
        )

    def operator(field, total_correlation):
        return (
            local_part(field)
            + (SHIFT / total) * times(total_correlation[:, :every], whole, ((1,), (0,)))
            + STRENGTH * times(total_correlation[:, every:], beta, ((1,), (0,)))
        )

    def dot(u, v):
        return jnp.sum(u * v, axis=1, keepdims=True)

    shaped = perturbation * occupied
    first, on_atoms, own, of_all = lax.psum(
        (
            times(shaped - SHIFT * start, whole, ((1,), (1,))),
            times(start, beta, ((1,), (1,))),
            times(occupied, pair, ((1,), (1,))),
            times(pair, whole, ((1,), (1,))),
        ),
        "dom",
    )
    own_radial, own_slope = own[:, 0:1], own[:, 1:2]
    first = first + STRENGTH * (own_radial * of_all[1:2] + own_slope * of_all[0:1])
    residual = (
        times(first * (1.0 / total), whole, ((1,), (0,)))
        - STRENGTH * times(on_atoms, beta, ((1,), (0,)))
        - local_part(start)
        - shaped
        - STRENGTH * (own_radial * pair[1:2] + own_slope * pair[0:1])
    )
    correlation, norm = lax.psum((correlate(residual), dot(residual, residual)), "dom")
    image = operator(residual, correlation)
    correlation, curve = lax.psum((correlate(image), dot(residual, image)), "dom")
    alpha = norm / curve
    again = operator(image, correlation)
    later = residual - alpha * image
    later_image = image - alpha * again
    new, bend, cross = lax.psum((dot(later, later), dot(later, later_image), dot(later, image)), "dom")
    ratio = new / norm
    step = new / (bend + ratio * (2.0 * cross + ratio * curve))
    answer = start + alpha * residual + step * (later + ratio * residual)
    return answer, later - step * (later_image + ratio * image)


def local(
    occupied,
    start_guess,
    potential,
    perturbation,
    band_energy,
    beta_radial,
    beta_slope,
    atom_owner,
    atom_site,
    sphere_offset,
    displaced,
):
    slabs = lax.axis_size("dom")
    beta, pair = atom_fields(
        slabs,
        start_guess.shape[2],
        beta_radial,
        beta_slope,
        sphere_offset,
        atom_owner,
        atom_site,
        displaced,
    )
    in_plane = jnp.asarray(plane_matrix())
    answer, residual = plain(
        occupied,
        start_guess[0],
        potential[None, :],
        perturbation,
        band_energy[:, None],
        beta,
        pair,
        in_plane,
    )
    return answer[None], residual[None]


def solution(mesh):
    return jax.shard_map(
        local,
        mesh=mesh,
        in_specs=(
            P("band", "dom"),
            P(None, "band", "dom"),
            P("dom"),
            P(None, "dom"),
            P("band"),
            P(),
            P(),
            P(),
            P(),
            P(),
            P(),
        ),
        out_specs=(P(None, "band", "dom"), P(None, "band", "dom")),
        check_vma=False,
    )
```

profile of v0, /device:TPU:0, one launch (start us, length us, event | category | flops | bytes accessed | tf_op | source)
XLA Modules:
  0.0 300.1 jit_solution(810453794440793870)
XLA Ops:
  7.2 0.0 all-gather.2.cloned.1.call-start
  7.2 0.7 all-gather.2.cloned.1.call-update
  7.9 0.0 all-reduce.7.cloned.1.call-start
  7.9 0.0 copy-start.9
  8.0 0.0 copy-start
  8.0 0.0 copy-start.1
  8.0 0.0 copy-start.2
  8.0 0.0 copy-start.3
  8.0 3.0 %collective-permute-start = (f32[64,1536]{1,0:T(8,128)}, f32[64,1536]{1,0:T(8,128)}, u32[]{:S(2)}, u32[]{:S(2)}) collective-permute-start(f32[64,1536]{1,0:T(8,128)} %bitcast.65), channel_id=1, source_target_pairs={{0,1},{1,2},{2,3},{3,4},{4,5},{5,6},{6,7},{7,0},{8,9},{9,10},{10,1... | collective-permute-start | bytes 1179656 | tf_op jit(solution)/shard_map/ppermute | solution.py:122
  11.0 3.1 %collective-permute-start.1 = (f32[64,1536]{1,0:T(8,128)}, f32[64,1536]{1,0:T(8,128)}, u32[]{:S(2)}, u32[]{:S(2)}) collective-permute-start(f32[64,1536]{1,0:T(8,128)} %bitcast.66), channel_id=1, source_target_pairs={{1,0},{2,1},{3,2},{4,3},{5,4},{6,5},{7,6},{0,7},{9,8},{10,9},{11,1... | collective-permute-start | bytes 1179656 | tf_op jit(solution)/shard_map/ppermute | solution.py:123
  14.1 1.1 reshape_squeeze.3
  15.3 0.0 copy-start.6
  16.0 2.0 convolution_bitcast_fusion
  18.0 0.2 copy.14
  18.1 0.1 reshape.21
  18.4 1.7 shard_map.131
  20.1 0.4 convolution_bitcast_fusion.2
  20.5 0.5 convolution_bitcast_fusion.1
  21.0 11.0 %all-gather.2.cloned.1.call-done = f32[256,1536]{1,0:T(8,128)} async-done(((f32[64,1536]{1,0:T(8,128)}), f32[256,1536]{1,0:T(8,128)}) %all-gather.2.cloned.1.call-update) | async-done | bytes 1572880 | tf_op jit(solution)/shard_map/all_gather | solution.py:116
  32.0 3.7 %fusion.85 = f32[64,256]{1,0:T(8,128)} fusion(f32[256,1536]{1,0:T(8,128)} %all-gather.2.cloned.1.call-done, f32[64,1536]{1,0:T(8,128)S(1)} %copy-done.7, f32[1536]{0:T(1024)S(1)} %reduce, f32[1,64,1536]{2,1,0:T(8,128)S(1)} %copy-done.6), kind=kOutput, calls=%fused_computation.158 | convolution fusion | flops 302284800 | bytes 2430976 | tf_op jit(solution)/shard_map/dot_general | solution.py:108
  35.7 0.0 all-reduce.7.cloned.1.call-update
  35.7 0.0 copy-start.10
  35.7 0.0 copy-start.11
  35.7 0.0 all-reduce.9.cloned.1.call-start
  35.8 1.3 fusion.119
  37.1 37.1 %all-reduce.2 = (f32[64,8]{0,1:T(8,128)S(1)}, f32[8,256]{1,0:T(8,128)S(1)}, f32[64,32]{0,1:T(8,128)S(1)}) all-reduce(f32[64,8]{0,1:T(8,128)S(1)} %convolution_bitcast_fusion.2, f32[8,256]{1,0:T(8,128)S(1)} %fusion.119, f32[64,32]{0,1:T(8,128)S(1)} %convolution_bitcast_fusion.1), channel_id=1, replica_groups=mesh['band'=4,'dom'=8] {'dom'}, use_global_device_ids=true, to_apply=%region_1.0 | all-reduce | flops 4608 | bytes 36864 | tf_op jit(solution)/shard_map/psum | solution.py:148
  74.2 30.3 %all-reduce.7.cloned.1.call-done = f32[64,256]{1,0:T(8,128)} async-done(((f32[64,256]{1,0:T(8,128)}), f32[64,256]{1,0:T(8,128)}) %all-reduce.7.cloned.1.call-update) | async-done | bytes 65552 | tf_op jit(solution)/shard_map/psum | solution.py:148
  104.5 1.9 fusion.95
  106.4 0.0 collective-permute-done
  106.4 0.0 collective-permute-done.1
  106.4 2.9 fusion.4
  109.4 0.5 fusion.122
  109.8 0.0 copy-start.8
  109.8 0.1 reshape.22
  109.9 3.3 %collective-permute-start.3 = (f32[64,1536]{1,0:T(8,128)S(1)}, f32[64,1536]{1,0:T(8,128)}, u32[]{:S(2)}, u32[]{:S(2)}) collective-permute-start(f32[64,1536]{1,0:T(8,128)S(1)} %fusion.4), channel_id=1, source_target_pairs={{1,0},{2,1},{3,2},{4,3},{5,4},{6,5},{7,6},{0,7},{9,8},{10,9},{11,1... | collective-permute-start | bytes 1179656 | tf_op jit(solution)/shard_map/ppermute | solution.py:123
  113.2 0.0 collective-permute-start.2
  113.2 1.6 fusion.121
  114.8 0.6 pad_maximum_fusion.6
  115.4 0.0 all-reduce.9.cloned.1.call-update
  115.5 0.2 all-reduce.11.cloned.1.call-start
  115.7 1.2 fusion.120
  116.9 1.9 reshape.23
  118.8 67.7 %all-reduce.9.cloned.1.call-done = f32[64,288]{1,0:T(8,128)} async-done(((f32[64,288]{1,0:T(8,128)}), f32[64,288]{1,0:T(8,128)}) %all-reduce.9.cloned.1.call-update) | async-done | bytes 73744 | tf_op jit(solution)/shard_map/psum | solution.py:166
  186.5 1.2 convolution_multiply_fusion.2
  187.7 0.0 collective-permute-done.3
  187.7 0.0 collective-permute-done.2
  187.7 3.5 %multiply_reduce_fusion.3 = (f32[64]{0:T(128)S(1)}, f32[64]{0:T(128)S(1)}, f32[64,1536]{1,0:T(8,128)S(1)}) fusion(f32[64,1536]{1,0:T(8,128)S(1)} %fusion.4, f32[64,1536]{1,0:T(8,128)S(1)} %convolution_multiply_fusion.2, f32[256,1536]{1,0:T(8,128)S(1)} %copy-done.5, f32[64,288]{1,0:T(8,128)} %all-reduce.9.cloned.1.call-done, f32[64]{0:T(128)S(1)} %copy-done.11, ...), kind=kOutput, calls=%fused_computation.156 | convolution fusion | flops 305725312 | bytes 4004608 | tf_op jit(solution)/shard_map/dot_general | solution.py:108
  191.2 0.5 fusion.125
  191.7 0.8 reshape.24
  192.5 2.4 collective-permute-start.5
  194.9 0.0 collective-permute-start.4
  194.9 1.6 fusion.124
  196.4 0.6 pad_maximum_fusion.7
  197.1 0.0 all-reduce.11.cloned.1.call-update
  197.1 2.2 fusion.123
  199.3 24.2 %all-reduce.1 = (f32[64,1]{0,1:T(1,128)S(1)}, f32[64,1]{0,1:T(1,128)S(1)}) all-reduce(f32[64,1]{0,1:T(1,128)S(1)} %bitcast.75, f32[64,1]{0,1:T(1,128)S(1)} %bitcast.74), channel_id=1, replica_groups=mesh['band'=4,'dom'=8] {'dom'}, use_global_device_ids=true, to_apply=%region_5.0 | all-reduce | flops 128 | bytes 1024 | tf_op jit(solution)/shard_map/psum | solution.py:166
  223.6 1.1 reshape.25
  224.7 43.4 %all-reduce.11.cloned.1.call-done = f32[64,288]{1,0:T(8,128)} async-done(((f32[64,288]{1,0:T(8,128)}), f32[64,288]{1,0:T(8,128)}) %all-reduce.11.cloned.1.call-update) | async-done | bytes 73744 | tf_op jit(solution)/shard_map/psum | solution.py:168
  268.1 1.9 convolution_multiply_fusion.1
  270.0 0.0 collective-permute-done.5
  270.0 0.0 collective-permute-done.4
  270.0 2.9 multiply_reduce_fusion
  272.9 19.5 %all-reduce = (f32[64,1]{0,1:T(1,128)S(1)}, f32[64,1]{0,1:T(1,128)S(1)}, f32[64,1]{0,1:T(1,128)S(1)}) all-reduce(f32[64,1]{0,1:T(1,128)S(1)} %bitcast.73, f32[64,1]{0,1:T(1,128)S(1)} %bitcast.72, f32[64,1]{0,1:T(1,128)S(1)} %bitcast.71), channel_id=1, replica_groups=mesh['band'=4,'dom'=8] {'dom'}, use_global_device_ids=true, to_apply=%region_10.0 | all-reduce | flops 192 | bytes 1536 | tf_op jit(solution)/shard_map/psum | solution.py:173
  292.4 1.1 subtract_bitcast_fusion
  (21 shorter events, 0.1 us)
Async XLA Ops:
  7.2 24.8 %all-gather.2.cloned.1.call-start = ((), (), s32[]{:S(2)}) async-start(), calls=%async_computation | async-start | bytes 1966080 | tf_op jit(solution)/shard_map/all_gather | solution.py:116
  7.9 96.6 %all-reduce.7.cloned.1.call-start = ((), (), s32[]{:S(2)}) async-start(), calls=%async_computation.1 | async-start | bytes 131072 | tf_op jit(solution)/shard_map/psum | solution.py:148
  7.9 10.3 %copy-start.9 = (f32[1,1536]{1,0:T(1,128)S(1)}, f32[1,1536]{1,0:T(1,128)}, u32[]{:S(2)}) copy-start(f32[1,1536]{1,0:T(1,128)} %param.15) | copy-start | bytes 18436
  8.0 10.4 %copy-start = (s32[3,512]{1,0:T(4,128)S(1)}, s32[3,512]{1,0:T(4,128)}, u32[]{:S(2)}) copy-start(s32[3,512]{1,0:T(4,128)} %offset.1) | copy-start | bytes 18436
  8.0 10.4 %copy-start.1 = (f32[512]{0:T(512)S(1)}, f32[512]{0:T(512)}, u32[]{:S(2)}) copy-start(f32[512]{0:T(512)} %param.17) | copy-start | bytes 6148
  8.0 10.4 %copy-start.2 = (f32[512]{0:T(512)S(1)}, f32[512]{0:T(512)}, u32[]{:S(2)}) copy-start(f32[512]{0:T(512)} %param.18) | copy-start | bytes 6148
  8.0 10.4 %copy-start.3 = (s32[3,32]{1,0:T(4,128)S(1)}, s32[3,32]{1,0:T(4,128)}, u32[]{:S(2)}) copy-start(s32[3,32]{1,0:T(4,128)} %site.1) | copy-start | bytes 1156
  8.0 10.4 %copy-start.4 = (s32[32]{0:T(128)S(1)}, s32[32]{0:T(128)}, u32[]{:S(2)}) copy-start(s32[32]{0:T(128)} %owner.1) | copy-start | bytes 388
  8.0 12.1 %copy-start.7 = (f32[64,1536]{1,0:T(8,128)S(1)}, f32[64,1536]{1,0:T(8,128)}, u32[]{:S(2)}) copy-start(f32[64,1536]{1,0:T(8,128)} %param.12) | copy-start | bytes 1179652
  8.0 98.4 %collective-permute-start = (f32[64,1536]{1,0:T(8,128)}, f32[64,1536]{1,0:T(8,128)}, u32[]{:S(2)}, u32[]{:S(2)}) collective-permute-start(f32[64,1536]{1,0:T(8,128)} %bitcast.65), channel_id=1, source_target_pairs={{0,1},{1,2},{2,3},{3,4},{4,5},{5,6},{6,7},{7,0},{8,9},{9,10},{10,1... | collective-permute-start | bytes 1179656 | tf_op jit(solution)/shard_map/ppermute | solution.py:122
  11.0 95.4 %collective-permute-start.1 = (f32[64,1536]{1,0:T(8,128)}, f32[64,1536]{1,0:T(8,128)}, u32[]{:S(2)}, u32[]{:S(2)}) collective-permute-start(f32[64,1536]{1,0:T(8,128)} %bitcast.66), channel_id=1, source_target_pairs={{1,0},{2,1},{3,2},{4,3},{5,4},{6,5},{7,6},{0,7},{9,8},{10,9},{11,1... | collective-permute-start | bytes 1179656 | tf_op jit(solution)/shard_map/ppermute | solution.py:123
  15.3 5.3 %copy-start.6 = (f32[1,64,1536]{2,1,0:T(8,128)S(1)}, f32[1,64,1536]{2,1,0:T(8,128)}, u32[]{:S(2)}) copy-start(f32[1,64,1536]{2,1,0:T(8,128)} %param.13) | copy-start | bytes 1179652
  31.9 3.8 %copy-start.5 = (f32[256,1536]{1,0:T(8,128)S(1)}, f32[256,1536]{1,0:T(8,128)}, u32[]{:S(2)}) copy-start(f32[256,1536]{1,0:T(8,128)} %all-gather.2.cloned.1.call-done) | copy-start | bytes 4718596
  35.7 70.7 %copy-start.10 = (f32[1536]{0:T(1024)S(1)}, f32[1536]{0:T(1024)}, u32[]{:S(2)}) copy-start(f32[1536]{0:T(1024)} %param.14) | copy-start | bytes 18436
  35.7 70.7 %copy-start.11 = (f32[64]{0:T(128)S(1)}, f32[64]{0:T(128)}, u32[]{:S(2)}) copy-start(f32[64]{0:T(128)} %param.16) | copy-start | bytes 772
  35.7 150.7 %all-reduce.9.cloned.1.call-start = ((), (), s32[]{:S(2)}) async-start(), calls=%async_computation.2 | async-start | bytes 196608 | tf_op jit(solution)/shard_map/psum | solution.py:166
  109.8 5.9 %copy-start.8 = (f32[256,256]{1,0:T(8,128)S(1)}, f32[256,256]{1,0:T(8,128)}, u32[]{:S(2)}) copy-start(f32[256,256]{1,0:T(8,128)} %constant.12.clone) | copy-start | bytes 786436
  109.9 77.8 %collective-permute-start.3 = (f32[64,1536]{1,0:T(8,128)S(1)}, f32[64,1536]{1,0:T(8,128)}, u32[]{:S(2)}, u32[]{:S(2)}) collective-permute-start(f32[64,1536]{1,0:T(8,128)S(1)} %fusion.4), channel_id=1, source_target_pairs={{1,0},{2,1},{3,2},{4,3},{5,4},{6,5},{7,6},{0,7},{9,8},{10,9},{11,1... | collective-permute-start | bytes 1179656 | tf_op jit(solution)/shard_map/ppermute | solution.py:123
  113.2 74.5 %collective-permute-start.2 = (f32[64,1536]{1,0:T(8,128)S(1)}, f32[64,1536]{1,0:T(8,128)}, u32[]{:S(2)}, u32[]{:S(2)}) collective-permute-start(f32[64,1536]{1,0:T(8,128)S(1)} %fusion.4), channel_id=1, source_target_pairs={{0,1},{1,2},{2,3},{3,4},{4,5},{5,6},{6,7},{7,0},{8,9},{9,10},{10,1... | collective-permute-start | bytes 1179656 | tf_op jit(solution)/shard_map/ppermute | solution.py:122
  115.5 152.6 %all-reduce.11.cloned.1.call-start = ((), (), s32[]{:S(2)}) async-start(), calls=%async_computation.3 | async-start | bytes 196608 | tf_op jit(solution)/shard_map/psum | solution.py:168
  192.5 77.5 %collective-permute-start.5 = (f32[64,1536]{1,0:T(8,128)S(1)}, f32[64,1536]{1,0:T(8,128)}, u32[]{:S(2)}, u32[]{:S(2)}) collective-permute-start(f32[64,1536]{1,0:T(8,128)S(1)} %get-tuple-element.29), channel_id=1, source_target_pairs={{1,0},{2,1},{3,2},{4,3},{5,4},{6,5},{7,6},{0,7},{9,8},{10,9},{11,1... | collective-permute-start | bytes 1179656 | tf_op jit(solution)/shard_map/ppermute | solution.py:123
  194.9 75.1 %collective-permute-start.4 = (f32[64,1536]{1,0:T(8,128)S(1)}, f32[64,1536]{1,0:T(8,128)}, u32[]{:S(2)}, u32[]{:S(2)}) collective-permute-start(f32[64,1536]{1,0:T(8,128)S(1)} %get-tuple-element.29), channel_id=1, source_target_pairs={{0,1},{1,2},{2,3},{3,4},{4,5},{5,6},{6,7},{7,0},{8,9},{9,10},{10,1... | collective-permute-start | bytes 1179656 | tf_op jit(solution)/shard_map/ppermute | solution.py:122
Sparse Core Ops, SparseCore 0:
  9.6 22.3 all-gather.1
  35.9 68.5 all-reduce.6
  115.6 70.8 all-reduce.8
  197.2 70.7 all-reduce.10
where the time goes:
time: 301 us; the launch traced here: 300 us
  waiting for transfers between devices  153 us (51%)
  blocking collectives  80.8 us (27%)
  matrix products  29.7 us (10%)
  between operations  14.8 us (5%)
  starting transfers between devices  12.2 us (4%)
  local copies, waits for them, and re-layouts  5.37 us (2%)
    psum x1, waiting for transfers between devices, plain(): lax.psum((correlate(residual), dot(residual, residual)), 'dom')  67.7 us
    psum x1, waiting for transfers between devices, plain(): lax.psum((correlate(image), dot(residual, image)), 'dom')  43.4 us
    psum x1, blocking collectives, plain(): lax.psum((times(shaped - SHIFT * start, whole, ((1,), (1,))), times(start...  37.1 us
    psum x1, waiting for transfers between devices, plain(): lax.psum((times(shaped - SHIFT * start, whole, ((1,), (1,))), times(start...  30.3 us
    dot_general x17, matrix products, times(): lax.dot_general(a, b, (dims, ((), ())), precision=HIGH, preferred_element...  29.7 us
    psum x1, blocking collectives, plain(): lax.psum((correlate(residual), dot(residual, residual)), 'dom')  24.2 us
    psum x1, blocking collectives, plain(): lax.psum((dot(later, later), dot(later, later_image), dot(later, image)),...  19.5 us
    all_gather x1, waiting for transfers between devices, plain(): whole = lax.all_gather(occupied, 'band', axis=0, tiled=True)  11 us
  transfers between devices with their start and end apart: 10, of which 4 were waited for; matrix products, arithmetic and copies ran while one was open for 8% of the time, Pallas kernels for 1%

commit v1 on v0

--- a/solution.py
+++ b/solution.py
@@ -41,8 +41,8 @@
     return (-KINETIC * full).astype(np.float32)
 
 
-def fields_kernel(slabs, depth, radial, slope, offset, owner, site, displaced, out, pair, padded):
-    atoms = out.shape[0]
+def fields_kernel(slabs, depth, radial, slope, offset, owner, site, displaced, out, padded):
+    atoms = owner.shape[0]
     planes = slabs * depth
     points = offset.shape[1]
     slab = lax.axis_index("dom")
@@ -75,15 +75,11 @@
         second = pltpu.roll(block, lax.rem(turn + PLANE - NX, PLANE), 1)
         return jnp.where(column >= x, first, second)
 
-    for a in range(atoms):
-        field = shifted(0, a)
+    out[atoms:, :] = jnp.zeros((out.shape[0] - atoms, out.shape[1]), jnp.float32)
+    for row in range(atoms + 2):
+        field = shifted(0, row) if row < atoms else shifted(row - atoms, displaced[0])
         for z in range(depth):
-            out[a : a + 1, z * PLANE : (z + 1) * PLANE] = field[z : z + 1]
-    pair[...] = jnp.zeros_like(pair)
-    for which in range(2):
-        field = shifted(which, displaced[0])
-        for z in range(depth):
-            pair[which : which + 1, z * PLANE : (z + 1) * PLANE] = field[z : z + 1]
+            out[row : row + 1, z * PLANE : (z + 1) * PLANE] = field[z : z + 1]
 
 
 def atom_fields(slabs, cells, beta_radial, beta_slope, offset, owner, site, displaced):
@@ -93,12 +89,9 @@
     smem = pl.BlockSpec(memory_space=pltpu.SMEM)
     return pl.pallas_call(
         functools.partial(fields_kernel, slabs, depth),
-        out_shape=(
-            jax.ShapeDtypeStruct((atoms, cells), jnp.float32),
-            jax.ShapeDtypeStruct((8, cells), jnp.float32),
-        ),
+        out_shape=jax.ShapeDtypeStruct((max(128, atoms + 16), cells), jnp.float32),
         in_specs=[vmem, vmem, vmem, smem, smem, smem],
-        out_specs=(vmem, vmem),
+        out_specs=vmem,
         scratch_shapes=[pltpu.VMEM((2, slabs * depth + 16, PLANE), jnp.float32)],
         compiler_params=pltpu.CompilerParams(vmem_limit_bytes=16 * 1024 * 1024),
     )(beta_radial[None, :], beta_slope[None, :], offset, owner, site, displaced)
@@ -175,6 +168,398 @@
     step = new / (bend + ratio * (2.0 * cross + ratio * curve))
     answer = start + alpha * residual + step * (later + ratio * residual)
     return answer, later - step * (later_image + ratio * image)
+
+
+NT = (((1,), (1,)), ((), ()))
+NN = (((1,), (0,)), ((), ()))
+MESH = pl.DeviceIdType.MESH
+
+
+def parts_of(x):
+    high = x.astype(jnp.bfloat16)
+    return high, (x - high.astype(jnp.float32)).astype(jnp.bfloat16)
+
+
+def product(a, b, dims):
+    def one(u, v):
+        return lax.dot_general(u, v, dims, preferred_element_type=jnp.float32)
+
+    return one(a[0], b[0]) + (one(a[0], b[1]) + one(a[1], b[0]))
+
+
+def fused_kernel(
+    atoms,
+    slabs,
+    occ,
+    start,
+    pot,
+    pert,
+    energy,
+    fields,
+    plane_high,
+    plane_low,
+    answer,
+    residual,
+    whole,
+    w_high,
+    w_low,
+    f_high,
+    f_low,
+    before,
+    after,
+    r0,
+    w0,
+    image,
+    part,
+    pieces,
+    summed,
+    totals,
+    rows_part,
+    rows_in,
+    last_part,
+    last_in,
+    band_send,
+    band_recv,
+    halo_send,
+    halo_recv,
+    sum_send,
+    sum_recv,
+    all_send,
+    all_recv,
+    rows_send,
+    rows_recv,
+    last_send,
+    last_recv,
+):
+    bands, cells = occ.shape
+    every = 4 * bands
+    total = cells * slabs
+    band = lax.axis_index("band")
+    slab = lax.axis_index("dom")
+    sibling = band + 1 - 2 * (band % 2)
+    across = (band + 2) % 4
+    barrier = pltpu.get_barrier_semaphore()
+    pl.semaphore_signal(barrier, inc=1, device_id={"band": sibling}, device_id_type=MESH)
+    pl.semaphore_signal(barrier, inc=1, device_id={"band": across}, device_id_type=MESH)
+    peers = [(slab + k) % slabs for k in range(slabs)]
+    for k in range(1, slabs):
+        pl.semaphore_signal(barrier, inc=1, device_id={"dom": peers[k]}, device_id_type=MESH)
+    pl.semaphore_wait(barrier, slabs + 1)
+
+    pending = []
+
+    def send(src, dst, send_sem, recv_sem, device):
+        copy = pltpu.make_async_remote_copy(
+            src_ref=src,
+            dst_ref=dst,
+            send_sem=send_sem,
+            recv_sem=recv_sem,
+            device_id=device,
+            device_id_type=MESH,
+        )
+        copy.start()
+        pending.append(copy)
+        return copy
+
+    def exchange_faces(turn, field):
+        return (
+            send(field, before.at[turn], halo_send.at[turn, 0], halo_recv.at[turn, 0], {"dom": peers[1]}),
+            send(
+                field, after.at[turn], halo_send.at[turn, 1], halo_recv.at[turn, 1], {"dom": peers[slabs - 1]}
+            ),
+        )
+
+    half = bands // 2
+    crossing = [
+        send(
+            occ.at[pl.ds(c * half, half)],
+            whole.at[1, pl.ds(c * half, half)],
+            band_send.at[c],
+            band_recv.at[c],
+            {"band": across},
+        )
+        for c in range(2)
+    ]
+    to_sibling = send(occ, whole.at[0], band_send.at[2], band_recv.at[2], {"band": sibling})
+    faces = exchange_faces(0, start)
+
+    def hold(row, block):
+        high, low = parts_of(block)
+        w_high[row : row + block.shape[0], :] = high
+        w_low[row : row + block.shape[0], :] = low
+
+    def hold_field(block):
+        high, low = parts_of(block)
+        f_high[...] = high
+        f_low[...] = low
+
+    def plane_image(field):
+        for z in range(HALO):
+            cut = slice(z * PLANE, (z + 1) * PLANE)
+            image[:, cut] = product(
+                (f_high[:, cut], f_low[:, cut]), (plane_high[...], plane_low[...]), NN
+            ) + (pot[:, cut] - energy[...]) * field[:, cut]
+
+    def across_planes(turn, field):
+        def group(i, carry):
+            rows = pl.ds(pl.multiple_of(i * 8, 8), 8)
+            grid = [
+                ref[rows, z * PLANE : (z + 1) * PLANE]
+                for ref in (before.at[turn], field, after.at[turn])
+                for z in range(HALO)
+            ]
+            for z in range(HALO):
+                cut = slice(z * PLANE, (z + 1) * PLANE)
+                value = image[rows, cut]
+                for d in range(1, 7):
+                    value += (-KINETIC * COEF[d]) * (grid[HALO + z - d] + grid[HALO + z + d])
+                image[rows, cut] = value
+            return carry
+
+        lax.fori_loop(0, bands // 8, group, 0)
+
+    def start_sum(turn):
+        return [
+            send(
+                part.at[turn, pl.ds(pl.multiple_of(peers[k] * 8, 8), 8)],
+                pieces.at[turn, k],
+                sum_send.at[turn, k],
+                sum_recv.at[turn, k],
+                {"dom": peers[k]},
+            )
+            for k in range(1, slabs)
+        ]
+
+    def share_sum(turn, copies):
+        mine = pl.ds(pl.multiple_of(slab * 8, 8), 8)
+        value = part[turn, mine, :]
+        for k in range(1, slabs):
+            copies[k - 1].wait_recv()
+            value += pieces[turn, k]
+        summed[turn] = value
+        shared = [
+            send(
+                summed.at[turn],
+                totals.at[turn, mine],
+                all_send.at[turn, k],
+                all_recv.at[turn, k],
+                {"dom": peers[k]},
+            )
+            for k in range(1, slabs)
+        ]
+        totals[turn, mine, :] = value
+        return shared
+
+    def finish_sum(shared):
+        for copy in shared:
+            copy.wait_recv()
+
+    lane = lax.broadcasted_iota(jnp.int32, (bands, 128), 1)
+
+    def correlate(rows):
+        return product((f_high[...], f_low[...]), (w_high[rows, :], w_low[rows, :]), NT)
+
+    def back(coefficients):
+        return product(parts_of(coefficients), (w_high[...], w_low[...]), NN)
+
+    hold(0, occ[...])
+    hold(every, fields[...])
+    hold_field(start[...])
+    plane_image(start)
+    ends = slice(every, every + 128)
+    on_start = correlate(ends)
+    on_own = product(
+        (w_high[0:bands, :], w_low[0:bands, :]), (w_high[ends, :], w_low[ends, :]), NT
+    )
+    part[0, :, every:] = jnp.where(lane < atoms, on_start, on_own)
+    shaped = pert[...] * occ[...]
+    hold_field(shaped - SHIFT * start[...])
+    to_sibling.wait_recv()
+    hold(bands, whole[0])
+    part[0, :, 0 : 2 * bands] = correlate(slice(0, 2 * bands))
+    passed = []
+    for c in range(2):
+        crossing[c].wait_recv()
+        passed.append(
+            send(
+                whole.at[1, pl.ds(c * half, half)],
+                whole.at[2, pl.ds(c * half, half)],
+                band_send.at[3 + c],
+                band_recv.at[3 + c],
+                {"band": sibling},
+            )
+        )
+    hold(2 * bands, whole[1])
+    for copy in passed:
+        copy.wait_recv()
+    hold(3 * bands, whole[2])
+    part[0, :, 2 * bands : every] = correlate(slice(2 * bands, every))
+    copies = start_sum(0)
+    pair = slice(every + atoms, every + atoms + 16)
+    rows_part[...] = product(
+        (w_high[pair, :], w_low[pair, :]), (w_high[0:every, :], w_low[0:every, :]), NT
+    )[0:8]
+    row_copies = [
+        send(rows_part, rows_in.at[k], rows_send.at[k], rows_recv.at[k], {"dom": peers[k]})
+        for k in range(1, slabs)
+    ]
+    shared = share_sum(0, copies)
+    for copy in faces:
+        copy.wait_recv()
+    across_planes(0, start)
+    of_all = rows_part[...]
+    for k in range(1, slabs):
+        row_copies[k - 1].wait_recv()
+        of_all += rows_in[k]
+    finish_sum(shared)
+    last = totals[0, :, every:]
+    own_radial, own_slope = last[:, atoms : atoms + 1], last[:, atoms + 1 : atoms + 2]
+    first = totals[0, :, 0:every] + STRENGTH * (own_radial * of_all[1:2] + own_slope * of_all[0:1])
+    ends_part = jnp.where(
+        lane < atoms,
+        last,
+        jnp.where(lane == atoms, own_slope, jnp.where(lane == atoms + 1, own_radial, 0.0)),
+    )
+    r0[...] = (
+        back(jnp.concatenate([first * (1.0 / total), -STRENGTH * ends_part], axis=1))
+        - image[...]
+        - pert[...] * occ[...]
+    )
+
+    def apply(turn, field, scalar):
+        faces = exchange_faces(turn, field)
+        hold_field(field[...])
+        part[turn, :, 0:every] = correlate(slice(0, every))
+        part[turn, :, every:] = jnp.where(lane == atoms, scalar, correlate(ends))
+        copies = start_sum(turn)
+        plane_image(field)
+        shared = share_sum(turn, copies)
+        for copy in faces:
+            copy.wait_recv()
+        across_planes(turn, field)
+        finish_sum(shared)
+        last = totals[turn, :, every:]
+        coefficients = jnp.concatenate(
+            [
+                totals[turn, :, 0:every] * (SHIFT / total),
+                jnp.where(lane < atoms, STRENGTH * last, 0.0),
+            ],
+            axis=1,
+        )
+        image[...] += back(coefficients)
+        return last[:, atoms : atoms + 1]
+
+    def dot(u, v):
+        return jnp.sum(u * v, axis=1, keepdims=True)
+
+    norm = apply(1, r0, dot(r0[...], r0[...]))
+    w0[...] = image[...]
+    curve = apply(2, w0, dot(r0[...], w0[...]))
+    alpha = norm / curve
+    later = r0[...] - alpha * w0[...]
+    later_image = w0[...] - alpha * image[...]
+    residual[0] = later
+    image[...] = later_image
+    three = jnp.where(
+        lane == 0,
+        dot(later, later),
+        jnp.where(
+            lane == 1, dot(later, later_image), jnp.where(lane == 2, dot(later, w0[...]), 0.0)
+        ),
+    )
+    eye = jnp.where(
+        lax.broadcasted_iota(jnp.int32, (128, 128), 0)
+        == lax.broadcasted_iota(jnp.int32, (128, 128), 1),
+        1.0,
+        0.0,
+    ).astype(jnp.float32)
+    three = jnp.concatenate([three, jnp.zeros((128 - bands, 128), jnp.float32)], axis=0)
+    last_part[...] = lax.dot_general(
+        eye[0:8], three, NT, precision=HIGH, preferred_element_type=jnp.float32
+    )
+    last_copies = [
+        send(last_part, last_in.at[k], last_send.at[k], last_recv.at[k], {"dom": peers[k]})
+        for k in range(1, slabs)
+    ]
+    value = last_part[...]
+    for k in range(1, slabs):
+        last_copies[k - 1].wait_recv()
+        value += last_in[k]
+    three = lax.dot_general(
+        eye[0:bands], value, NT, precision=HIGH, preferred_element_type=jnp.float32
+    )
+    new, bend, cross = three[:, 0:1], three[:, 1:2], three[:, 2:3]
+    ratio = new / norm
+    step = new / (bend + ratio * (2.0 * cross + ratio * curve))
+    later = residual[0]
+    answer[0] = start[...] + alpha * r0[...] + step * (later + ratio * r0[...])
+    residual[0] = later - step * (image[...] + ratio * w0[...])
+    for copy in pending:
+        copy.wait_send()
+
+
+def fused(atoms, occupied, start_guess, potential, perturbation, energy, fields, in_plane):
+    slabs = lax.axis_size("dom")
+    bands, cells = occupied.shape
+    every = 4 * bands
+    rows = every + 128
+    plane_high = in_plane.astype(jnp.bfloat16)
+    plane_low = (in_plane - plane_high.astype(np.float32)).astype(jnp.bfloat16)
+    f32, bf16 = jnp.float32, jnp.bfloat16
+    vmem = pl.BlockSpec(memory_space=pltpu.VMEM)
+    out = jax.ShapeDtypeStruct((1, bands, cells), f32)
+    dma = pltpu.SemaphoreType.DMA
+    field = pltpu.VMEM((bands, cells), f32)
+    return pl.pallas_call(
+        functools.partial(fused_kernel, atoms, slabs),
+        out_shape=(out, out),
+        in_specs=[vmem] * 8,
+        out_specs=(vmem, vmem),
+        scratch_shapes=[
+            pltpu.VMEM((3, bands, cells), f32),
+            pltpu.VMEM((rows, cells), bf16),
+            pltpu.VMEM((rows, cells), bf16),
+            pltpu.VMEM((bands, cells), bf16),
+            pltpu.VMEM((bands, cells), bf16),
+            pltpu.VMEM((3, bands, cells), f32),
+            pltpu.VMEM((3, bands, cells), f32),
+            field,
+            field,
+            field,
+            pltpu.VMEM((3, bands, rows), f32),
+            pltpu.VMEM((3, slabs, 8, rows), f32),
+            pltpu.VMEM((3, 8, rows), f32),
+            pltpu.VMEM((3, bands, rows), f32),
+            pltpu.VMEM((8, every), f32),
+            pltpu.VMEM((slabs, 8, every), f32),
+            pltpu.VMEM((8, 128), f32),
+            pltpu.VMEM((slabs, 8, 128), f32),
+            dma((5,)),
+            dma((5,)),
+            dma((3, 2)),
+            dma((3, 2)),
+            dma((3, slabs)),
+            dma((3, slabs)),
+            dma((3, slabs)),
+            dma((3, slabs)),
+            dma((slabs,)),
+            dma((slabs,)),
+            dma((slabs,)),
+            dma((slabs,)),
+        ],
+        compiler_params=pltpu.CompilerParams(
+            collective_id=0, has_side_effects=True, vmem_limit_bytes=40 * 1024 * 1024
+        ),
+    )(
+        occupied,
+        start_guess[0],
+        potential,
+        perturbation,
+        energy,
+        fields,
+        jnp.asarray(plane_high),
+        jnp.asarray(plane_low),
+    )
 
 
 def local(
@@ -191,26 +576,33 @@
     displaced,
 ):
     slabs = lax.axis_size("dom")
-    beta, pair = atom_fields(
-        slabs,
-        start_guess.shape[2],
-        beta_radial,
-        beta_slope,
-        sphere_offset,
-        atom_owner,
-        atom_site,
-        displaced,
-    )
-    in_plane = jnp.asarray(plane_matrix())
+    bands, cells = start_guess.shape[1:]
+    atoms = atom_owner.shape[0]
+    fields = atom_fields(
+        slabs, cells, beta_radial, beta_slope, sphere_offset, atom_owner, atom_site, displaced
+    )
+    in_plane = plane_matrix()
+    fits = bands == 8 * slabs and lax.axis_size("band") == 4 and atoms % 16 == 0 and atoms <= 112
+    if fits and cells == HALO * PLANE:
+        return fused(
+            atoms,
+            occupied,
+            start_guess,
+            potential[None, :],
+            perturbation,
+            band_energy[:, None],
+            fields,
+            in_plane,
+        )
     answer, residual = plain(
         occupied,
         start_guess[0],
         potential[None, :],
         perturbation,
         band_energy[:, None],
-        beta,
-        pair,
-        in_plane,
+        fields[:atoms],
+        fields[atoms : atoms + 8],
+        jnp.asarray(in_plane),
     )
     return answer[None], residual[None]
 

time: 301 us -> 94.1 us (0.31)
  waiting for transfers between devices: 153 us -> 0 us
  Pallas kernels: 1.71 us -> 87.8 us
  blocking collectives: 80.8 us -> 0 us
  matrix products: 29.7 us -> 0 us
  between operations: 14.8 us -> 1.36 us
  starting transfers between devices: 12.2 us -> 0 us
    psum x3 -> x0, waiting for transfers between devices: 141 us -> none  [the longest x1 67.7 us: plain(): lax.psum((correlate(residual), dot(residual, residual)), 'dom')]
    pallas_call x0 -> x1, Pallas kernels: none -> 86 us  [fused(): pl.pallas_call(functools.partial(fused_kernel, atoms, slabs), out_shape=(...]
    psum x3 -> x0, blocking collectives: 80.8 us -> none  [the longest x1 37.1 us: plain(): lax.psum((times(shaped - SHIFT * start, whole, ((1,), (1,))), times(start...]
    dot_general x17 -> x0, matrix products: 29.7 us -> none  [times(): lax.dot_general(a, b, (dims, ((), ())), precision=HIGH, preferred_element...]
    ppermute x6 -> x0, starting transfers between devices: 11.8 us -> none  [the longest x3 8.8 us: local_part(): after = lax.ppermute(field, 'dom', down)]
    all_gather x1 -> x0, waiting for transfers between devices: 11 us -> none  [plain(): whole = lax.all_gather(occupied, 'band', axis=0, tiled=True)]
    unnamed x24 -> x26, local copies, waits for them, and re-layouts: 0.06 us -> 4.61 us
    reshape x5 -> x0, local copies, waits for them, and re-layouts: 4 us -> none  [the longest x3 3.08 us: local_part(): times(field.reshape(bands * depth, PLANE), in_plane, ((1,), (0,)))]
  transfers between devices with their start and end apart: 10 -> 0, of which waited for: 4 -> 0; matrix products, arithmetic and copies ran while one was open for 8% -> 0% of each run, Pallas kernels for 1% -> 0%
where the time goes in v1:
time: 94.1 us; the launch traced here: 93.8 us
  Pallas kernels  87.8 us (93%)
  local copies, waits for them, and re-layouts  4.71 us (5%)
  between operations  1.36 us (1%)
    pallas_call x1, Pallas kernels, fused(): pl.pallas_call(functools.partial(fused_kernel, atoms, slabs), out_shape=(...  86 us
    unnamed x26, local copies, waits for them, and re-layouts  4.61 us

profile of v1, /device:TPU:0, one launch (start us, length us, event | category | flops | bytes accessed | tf_op | source)
XLA Modules:
  0.0 93.8 jit_solution(10563239363774855675)
XLA Ops:
  0.6 0.0 copy-start.10
  1.3 0.0 copy-done.10
  1.3 0.0 copy-start.11
  1.3 0.6 copy-done.11
  2.0 0.0 copy-start.4
  2.0 0.0 copy-start.6
  2.0 0.0 copy-start.7
  2.0 0.0 copy-start.8
  2.0 0.0 copy-start.9
  2.0 0.1 copy.15.energy
  2.1 0.6 copy-done.4
  2.7 0.0 copy-done.6
  2.7 0.0 copy-done.7
  2.7 0.0 copy-done.8
  2.7 0.0 copy-done.9
  2.7 0.0 copy-start
  2.7 0.0 copy-start.1
  2.7 0.0 copy-start.5
  2.7 1.7 %shard_map.140.fields = f32[128,1536]{1,0:T(8,128)S(1)} custom-call(f32[1,512]{1,0:T(1,128)S(1)} %bitcast.5, f32[1,512]{1,0:T(1,128)S(1)} %bitcast.6, s32[3,512]{1,0:T(4,128)S(1)} %copy-done.4, s32[32]{0:T(128)S(1)} %copy-done.9, s32[3,32]{1,0:T(4,128)S(1)} %copy-done.8, s32[1]{0:T(128)S(6)} %copy.18.displaced), custom_call_target="tpu_custom_call" | custom-call | tf_op jit(solution)/shard_map/pallas_call | solution.py:90
  4.5 0.0 copy-done
  4.5 0.0 copy-done.1
  4.5 0.0 copy-done.5
  4.5 0.0 copy-start.2
  4.5 0.9 copy-done.2
  5.4 0.0 copy-start.3
  5.4 0.9 copy-done.3
  6.3 86.0 %shard_map.141 = (f32[1,64,1536]{2,1,0:T(8,128)S(1)}, f32[1,64,1536]{2,1,0:T(8,128)S(1)}) custom-call(f32[64,1536]{1,0:T(8,128)S(1)} %copy-done, f32[64,1536]{1,0:T(8,128)S(1)} %bitcast.4, f32[1,1536]{1,0:T(1,128)S(1)} %broadcast_in_dim.12.pot, f32[1,1536]{1,0:T(1,128)S(1)} %copy-done.5, f32[64,1]{1,0:T(8,128)S(1)} %copy.15.energy, ...), custom_call_target="tpu_custom_call" | custom-call | tf_op jit(solution)/shard_map/pallas_call | solution.py:513
  92.3 0.7 copy.19
  93.1 0.7 copy.20
  (1 shorter events, 0.0 us)
Async XLA Ops:
  0.6 0.7 copy-start.10
  1.3 0.7 copy-start.11
  2.0 0.7 copy-start.4
  2.0 0.7 copy-start.6
  2.0 0.7 copy-start.7
  2.0 0.7 copy-start.8
  2.0 0.7 copy-start.9
  2.7 1.8 %copy-start = (f32[64,1536]{1,0:T(8,128)S(1)}, f32[64,1536]{1,0:T(8,128)}, u32[]{:S(2)}) copy-start(f32[64,1536]{1,0:T(8,128)} %occ.1) | copy-start | bytes 1179652
  2.7 1.8 %copy-start.1 = (f32[1,64,1536]{2,1,0:T(8,128)S(1)}, f32[1,64,1536]{2,1,0:T(8,128)}, u32[]{:S(2)}) copy-start(f32[1,64,1536]{2,1,0:T(8,128)} %param.14) | copy-start | bytes 1179652
  2.7 1.8 %copy-start.5 = (f32[1,1536]{1,0:T(1,128)S(1)}, f32[1,1536]{1,0:T(1,128)}, u32[]{:S(2)}) copy-start(f32[1,1536]{1,0:T(1,128)} %pert.1) | copy-start | bytes 18436
  4.5 0.9 copy-start.2
  5.4 0.9 copy-start.3

commit v2 on v1

--- a/solution.py
+++ b/solution.py
@@ -11,6 +11,7 @@
 NX = 16
 PLANE = NY * NX
 HALO = 6
+CHUNKS = 4
 RAD = 5
 
 COEF = (
@@ -205,8 +206,7 @@
     w_low,
     f_high,
     f_low,
-    before,
-    after,
+    faces,
     r0,
     w0,
     image,
@@ -220,8 +220,10 @@
     last_in,
     band_send,
     band_recv,
-    halo_send,
-    halo_recv,
+    face_send,
+    face_recv,
+    hand_send,
+    hand_recv,
     sum_send,
     sum_recv,
     all_send,
@@ -261,12 +263,34 @@
         pending.append(copy)
         return copy
 
-    def exchange_faces(turn, field):
-        return (
-            send(field, before.at[turn], halo_send.at[turn, 0], halo_recv.at[turn, 0], {"dom": peers[1]}),
+    chunk = bands // CHUNKS
+    side = slab % 2
+    beside = slab + 1 - 2 * side
+    beyond = (slab + slabs + 2 - 4 * side) % slabs
+
+    def send_face(turn, field):
+        return [
             send(
-                field, after.at[turn], halo_send.at[turn, 1], halo_recv.at[turn, 1], {"dom": peers[slabs - 1]}
-            ),
+                field.at[pl.ds(c * chunk, chunk)],
+                faces.at[turn, side, pl.ds(c * chunk, chunk)],
+                face_send.at[turn, c],
+                face_recv.at[turn, c],
+                {"dom": beside},
+            )
+            for c in range(CHUNKS)
+        ]
+
+    def hand_on(turn, copies, c):
+        copies[c].wait_recv()
+        block = faces.at[turn, 1 - side, pl.ds(c * chunk, chunk)]
+        copies.append(
+            send(
+                block,
+                faces.at[turn, side, pl.ds(c * chunk, chunk)],
+                hand_send.at[turn, c],
+                hand_recv.at[turn, c],
+                {"dom": beyond},
+            )
         )
 
     half = bands // 2
@@ -281,7 +305,7 @@
         for c in range(2)
     ]
     to_sibling = send(occ, whole.at[0], band_send.at[2], band_recv.at[2], {"band": sibling})
-    faces = exchange_faces(0, start)
+    moving = send_face(0, start)
 
     def hold(row, block):
         high, low = parts_of(block)
@@ -293,19 +317,21 @@
         f_high[...] = high
         f_low[...] = low
 
-    def plane_image(field):
-        for z in range(HALO):
+    def plane_image(field, planes):
+        for z in planes:
             cut = slice(z * PLANE, (z + 1) * PLANE)
             image[:, cut] = product(
                 (f_high[:, cut], f_low[:, cut]), (plane_high[...], plane_low[...]), NN
             ) + (pot[:, cut] - energy[...]) * field[:, cut]
 
-    def across_planes(turn, field):
+    def across_planes(turn, field, copies, c):
+        copies[CHUNKS + c].wait_recv()
+
         def group(i, carry):
             rows = pl.ds(pl.multiple_of(i * 8, 8), 8)
             grid = [
                 ref[rows, z * PLANE : (z + 1) * PLANE]
-                for ref in (before.at[turn], field, after.at[turn])
+                for ref in (faces.at[turn, 0], field, faces.at[turn, 1])
                 for z in range(HALO)
             ]
             for z in range(HALO):
@@ -316,7 +342,7 @@
                 image[rows, cut] = value
             return carry
 
-        lax.fori_loop(0, bands // 8, group, 0)
+        lax.fori_loop(c * chunk // 8, (c + 1) * chunk // 8, group, 0)
 
     def start_sum(turn):
         return [
@@ -365,13 +391,15 @@
     hold(0, occ[...])
     hold(every, fields[...])
     hold_field(start[...])
-    plane_image(start)
+    plane_image(start, range(HALO))
+    hand_on(0, moving, 0)
     ends = slice(every, every + 128)
     on_start = correlate(ends)
     on_own = product(
         (w_high[0:bands, :], w_low[0:bands, :]), (w_high[ends, :], w_low[ends, :]), NT
     )
     part[0, :, every:] = jnp.where(lane < atoms, on_start, on_own)
+    hand_on(0, moving, 1)
     shaped = pert[...] * occ[...]
     hold_field(shaped - SHIFT * start[...])
     to_sibling.wait_recv()
@@ -379,6 +407,7 @@
     part[0, :, 0 : 2 * bands] = correlate(slice(0, 2 * bands))
     passed = []
     for c in range(2):
+        hand_on(0, moving, 2 + c)
         crossing[c].wait_recv()
         passed.append(
             send(
@@ -404,9 +433,8 @@
         for k in range(1, slabs)
     ]
     shared = share_sum(0, copies)
-    for copy in faces:
-        copy.wait_recv()
-    across_planes(0, start)
+    for c in range(CHUNKS):
+        across_planes(0, start, moving, c)
     of_all = rows_part[...]
     for k in range(1, slabs):
         row_copies[k - 1].wait_recv()
@@ -427,16 +455,21 @@
     )
 
     def apply(turn, field, scalar):
-        faces = exchange_faces(turn, field)
+        moving = send_face(turn, field)
         hold_field(field[...])
-        part[turn, :, 0:every] = correlate(slice(0, every))
         part[turn, :, every:] = jnp.where(lane == atoms, scalar, correlate(ends))
+        hand_on(turn, moving, 0)
+        part[turn, :, 0 : every // 2] = correlate(slice(0, every // 2))
+        hand_on(turn, moving, 1)
+        part[turn, :, every // 2 : every] = correlate(slice(every // 2, every))
         copies = start_sum(turn)
-        plane_image(field)
+        hand_on(turn, moving, 2)
+        plane_image(field, range(0, HALO // 2))
+        hand_on(turn, moving, 3)
+        plane_image(field, range(HALO // 2, HALO))
         shared = share_sum(turn, copies)
-        for copy in faces:
-            copy.wait_recv()
-        across_planes(turn, field)
+        for c in range(CHUNKS):
+            across_planes(turn, field, moving, c)
         finish_sum(shared)
         last = totals[turn, :, every:]
         coefficients = jnp.concatenate(
@@ -521,8 +554,7 @@
             pltpu.VMEM((rows, cells), bf16),
             pltpu.VMEM((bands, cells), bf16),
             pltpu.VMEM((bands, cells), bf16),
-            pltpu.VMEM((3, bands, cells), f32),
-            pltpu.VMEM((3, bands, cells), f32),
+            pltpu.VMEM((3, 2, bands, cells), f32),
             field,
             field,
             field,
@@ -536,8 +568,10 @@
             pltpu.VMEM((slabs, 8, 128), f32),
             dma((5,)),
             dma((5,)),
-            dma((3, 2)),
-            dma((3, 2)),
+            dma((3, CHUNKS)),
+            dma((3, CHUNKS)),
+            dma((3, CHUNKS)),
+            dma((3, CHUNKS)),
             dma((3, slabs)),
             dma((3, slabs)),
             dma((3, slabs)),

time: 94.1 us -> 85.1 us (0.904)
  Pallas kernels: 87.8 us -> 78.8 us
    pallas_call x1, Pallas kernels: 86 us -> 77 us  [fused(): pl.pallas_call(functools.partial(fused_kernel, atoms, slabs), out_shape=(...]
where the time goes in v2:
time: 85.1 us; the launch traced here: 84.8 us
  Pallas kernels  78.8 us (93%)
  local copies, waits for them, and re-layouts  4.71 us (6%)
  between operations  1.36 us (2%)
    pallas_call x1, Pallas kernels, fused(): pl.pallas_call(functools.partial(fused_kernel, atoms, slabs), out_shape=(...  77 us
    unnamed x26, local copies, waits for them, and re-layouts  4.61 us
    pallas_call x1, Pallas kernels, atom_fields(): pl.pallas_call(functools.partial(fields_kernel, slabs, depth), out_shape=...  1.75 us

profile of v2, /device:TPU:0, one launch (start us, length us, event | category | flops | bytes accessed | tf_op | source)
XLA Modules:
  0.0 84.8 jit_solution(3652745117061838753)
XLA Ops:
  0.6 0.0 copy-start.10
  1.3 0.0 copy-done.10
  1.3 0.0 copy-start.11
  1.3 0.6 copy-done.11
  2.0 0.0 copy-start.4
  2.0 0.0 copy-start.6
  2.0 0.0 copy-start.7
  2.0 0.0 copy-start.8
  2.0 0.0 copy-start.9
  2.0 0.1 copy.15.energy
  2.1 0.6 copy-done.4
  2.7 0.0 copy-done.6
  2.7 0.0 copy-done.7
  2.7 0.0 copy-done.8
  2.7 0.0 copy-done.9
  2.7 0.0 copy-start
  2.7 0.0 copy-start.1
  2.7 0.0 copy-start.5
  2.7 1.7 %shard_map.140.fields = f32[128,1536]{1,0:T(8,128)S(1)} custom-call(f32[1,512]{1,0:T(1,128)S(1)} %bitcast.5, f32[1,512]{1,0:T(1,128)S(1)} %bitcast.6, s32[3,512]{1,0:T(4,128)S(1)} %copy-done.4, s32[32]{0:T(128)S(1)} %copy-done.9, s32[3,32]{1,0:T(4,128)S(1)} %copy-done.8, s32[1]{0:T(128)S(6)} %copy.18.displaced), custom_call_target="tpu_custom_call" | custom-call | tf_op jit(solution)/shard_map/pallas_call | solution.py:91
  4.5 0.0 copy-done
  4.5 0.0 copy-done.1
  4.5 0.0 copy-done.5
  4.5 0.0 copy-start.2
  4.5 0.9 %copy-done.2 = bf16[256,256]{1,0:T(8,128)(2,1)S(1)} copy-done((bf16[256,256]{1,0:T(8,128)(2,1)S(1)}, bf16[256,256]{1,0:T(8,128)(2,1)}, u32[]{:S(2)}) %copy-start.2) | copy-done | bytes 131096
  5.4 0.0 copy-start.3
  5.4 0.9 %copy-done.3 = bf16[256,256]{1,0:T(8,128)(2,1)S(1)} copy-done((bf16[256,256]{1,0:T(8,128)(2,1)S(1)}, bf16[256,256]{1,0:T(8,128)(2,1)}, u32[]{:S(2)}) %copy-start.3) | copy-done | bytes 131096
  6.3 77.0 %shard_map.141 = (f32[1,64,1536]{2,1,0:T(8,128)S(1)}, f32[1,64,1536]{2,1,0:T(8,128)S(1)}) custom-call(f32[64,1536]{1,0:T(8,128)S(1)} %copy-done, f32[64,1536]{1,0:T(8,128)S(1)} %bitcast.4, f32[1,1536]{1,0:T(1,128)S(1)} %broadcast_in_dim.12.pot, f32[1,1536]{1,0:T(1,128)S(1)} %copy-done.5, f32[64,1]{1,0:T(8,128)S(1)} %copy.15.energy, ...), custom_call_target="tpu_custom_call" | custom-call | tf_op jit(solution)/shard_map/pallas_call | solution.py:546
  83.3 0.7 copy.19
  84.1 0.7 copy.20
  (1 shorter events, 0.0 us)
Async XLA Ops:
  0.6 0.7 copy-start.10
  1.3 0.7 copy-start.11
  2.0 0.7 copy-start.4
  2.0 0.7 copy-start.6
  2.0 0.7 copy-start.7
  2.0 0.7 copy-start.8
  2.0 0.7 copy-start.9
  2.7 1.8 %copy-start = (f32[64,1536]{1,0:T(8,128)S(1)}, f32[64,1536]{1,0:T(8,128)}, u32[]{:S(2)}) copy-start(f32[64,1536]{1,0:T(8,128)} %occ.1) | copy-start | bytes 1179652
  2.7 1.8 %copy-start.1 = (f32[1,64,1536]{2,1,0:T(8,128)S(1)}, f32[1,64,1536]{2,1,0:T(8,128)}, u32[]{:S(2)}) copy-start(f32[1,64,1536]{2,1,0:T(8,128)} %param.14) | copy-start | bytes 1179652
  2.7 1.8 %copy-start.5 = (f32[1,1536]{1,0:T(1,128)S(1)}, f32[1,1536]{1,0:T(1,128)}, u32[]{:S(2)}) copy-start(f32[1,1536]{1,0:T(1,128)} %pert.1) | copy-start | bytes 18436
  4.5 0.9 %copy-start.2 = (bf16[256,256]{1,0:T(8,128)(2,1)S(1)}, bf16[256,256]{1,0:T(8,128)(2,1)}, u32[]{:S(2)}) copy-start(bf16[256,256]{1,0:T(8,128)(2,1)} %constant.5.clone.plane_low) | copy-start | bytes 393220
  5.4 0.9 %copy-start.3 = (bf16[256,256]{1,0:T(8,128)(2,1)S(1)}, bf16[256,256]{1,0:T(8,128)(2,1)}, u32[]{:S(2)}) copy-start(bf16[256,256]{1,0:T(8,128)(2,1)} %constant.4.clone.plane_high) | copy-start | bytes 393220

commit v3 on v2

--- a/solution.py
+++ b/solution.py
@@ -11,7 +11,8 @@
 NX = 16
 PLANE = NY * NX
 HALO = 6
-CHUNKS = 4
+CHUNKS = 8
+SUM_AT = 3
 RAD = 5
 
 COEF = (
@@ -191,16 +192,18 @@
 def fused_kernel(
     atoms,
     slabs,
-    occ,
-    start,
+    occ_in,
+    start_in,
     pot,
     pert,
     energy,
     fields,
+    answer,
+    residual,
+    occ,
+    start,
     plane_high,
     plane_low,
-    answer,
-    residual,
     whole,
     w_high,
     w_low,
@@ -232,6 +235,7 @@
     rows_recv,
     last_send,
     last_recv,
+    local_sem,
 ):
     bands, cells = occ.shape
     every = 4 * bands
@@ -240,6 +244,12 @@
     slab = lax.axis_index("dom")
     sibling = band + 1 - 2 * (band % 2)
     across = (band + 2) % 4
+    loads = [
+        pltpu.make_async_copy(occ_in, occ, local_sem.at[0]),
+        pltpu.make_async_copy(start_in, start, local_sem.at[1]),
+    ]
+    for load in loads:
+        load.start()
     barrier = pltpu.get_barrier_semaphore()
     pl.semaphore_signal(barrier, inc=1, device_id={"band": sibling}, device_id_type=MESH)
     pl.semaphore_signal(barrier, inc=1, device_id={"band": across}, device_id_type=MESH)
@@ -268,35 +278,32 @@
     beside = slab + 1 - 2 * side
     beyond = (slab + slabs + 2 - 4 * side) % slabs
 
-    def send_face(turn, field):
-        return [
-            send(
-                field.at[pl.ds(c * chunk, chunk)],
-                faces.at[turn, side, pl.ds(c * chunk, chunk)],
-                face_send.at[turn, c],
-                face_recv.at[turn, c],
-                {"dom": beside},
-            )
-            for c in range(CHUNKS)
-        ]
+    def send_face(turn, field, c):
+        return send(
+            field.at[pl.ds(c * chunk, chunk)],
+            faces.at[turn, side, pl.ds(c * chunk, chunk)],
+            face_send.at[turn, c],
+            face_recv.at[turn, c],
+            {"dom": beside},
+        )
+
+    def hand_over(turn, c):
+        return send(
+            faces.at[turn, 1 - side, pl.ds(c * chunk, chunk)],
+            faces.at[turn, side, pl.ds(c * chunk, chunk)],
+            hand_send.at[turn, c],
+            hand_recv.at[turn, c],
+            {"dom": beyond},
+        )
 
     def hand_on(turn, copies, c):
         copies[c].wait_recv()
-        block = faces.at[turn, 1 - side, pl.ds(c * chunk, chunk)]
-        copies.append(
-            send(
-                block,
-                faces.at[turn, side, pl.ds(c * chunk, chunk)],
-                hand_send.at[turn, c],
-                hand_recv.at[turn, c],
-                {"dom": beyond},
-            )
-        )
+        copies.append(hand_over(turn, c))
 
     half = bands // 2
     crossing = [
         send(
-            occ.at[pl.ds(c * half, half)],
+            occ_in.at[pl.ds(c * half, half)],
             whole.at[1, pl.ds(c * half, half)],
             band_send.at[c],
             band_recv.at[c],
@@ -304,8 +311,8 @@
         )
         for c in range(2)
     ]
-    to_sibling = send(occ, whole.at[0], band_send.at[2], band_recv.at[2], {"band": sibling})
-    moving = send_face(0, start)
+    to_sibling = send(occ_in, whole.at[0], band_send.at[2], band_recv.at[2], {"band": sibling})
+    moving = [send_face(0, start_in, c) for c in range(CHUNKS)]
 
     def hold(row, block):
         high, low = parts_of(block)
@@ -324,9 +331,7 @@
                 (f_high[:, cut], f_low[:, cut]), (plane_high[...], plane_low[...]), NN
             ) + (pot[:, cut] - energy[...]) * field[:, cut]
 
-    def across_planes(turn, field, copies, c):
-        copies[CHUNKS + c].wait_recv()
-
+    def across_planes(turn, field, c):
         def group(i, carry):
             rows = pl.ds(pl.multiple_of(i * 8, 8), 8)
             grid = [
@@ -388,26 +393,43 @@
     def back(coefficients):
         return product(parts_of(coefficients), (w_high[...], w_low[...]), NN)
 
+    one_cell = lax.broadcasted_iota(jnp.int32, (PLANE, PLANE), 0)
+    other_cell = lax.broadcasted_iota(jnp.int32, (PLANE, PLANE), 1)
+    along_x = (one_cell - other_cell) & (NX - 1)
+    along_y = ((one_cell >> 4) - (other_cell >> 4)) & (NY - 1)
+    away_x = jnp.minimum(along_x, NX - along_x)
+    away_y = jnp.minimum(along_y, NY - along_y)
+    away = jnp.where(away_x == 0, away_y, jnp.where(away_y == 0, away_x, NX))
+    matrix = jnp.where(away == 0, -KINETIC * 3.0 * COEF[0], 0.0)
+    for d in range(1, 7):
+        matrix = jnp.where(away == d, -KINETIC * COEF[d], matrix)
+    matrix_high, matrix_low = parts_of(matrix.astype(jnp.float32))
+    plane_high[...] = matrix_high
+    plane_low[...] = matrix_low
+
+    for load in loads:
+        load.wait()
     hold(0, occ[...])
     hold(every, fields[...])
     hold_field(start[...])
     plane_image(start, range(HALO))
     hand_on(0, moving, 0)
+    hand_on(0, moving, 1)
     ends = slice(every, every + 128)
     on_start = correlate(ends)
     on_own = product(
         (w_high[0:bands, :], w_low[0:bands, :]), (w_high[ends, :], w_low[ends, :]), NT
     )
     part[0, :, every:] = jnp.where(lane < atoms, on_start, on_own)
-    hand_on(0, moving, 1)
+    hand_on(0, moving, 2)
     shaped = pert[...] * occ[...]
     hold_field(shaped - SHIFT * start[...])
     to_sibling.wait_recv()
     hold(bands, whole[0])
+    hand_on(0, moving, 3)
     part[0, :, 0 : 2 * bands] = correlate(slice(0, 2 * bands))
     passed = []
     for c in range(2):
-        hand_on(0, moving, 2 + c)
         crossing[c].wait_recv()
         passed.append(
             send(
@@ -418,6 +440,8 @@
                 {"band": sibling},
             )
         )
+        hand_on(0, moving, 4 + 2 * c)
+        hand_on(0, moving, 5 + 2 * c)
     hold(2 * bands, whole[1])
     for copy in passed:
         copy.wait_recv()
@@ -434,7 +458,8 @@
     ]
     shared = share_sum(0, copies)
     for c in range(CHUNKS):
-        across_planes(0, start, moving, c)
+        moving[CHUNKS + c].wait_recv()
+        across_planes(0, start, c)
     of_all = rows_part[...]
     for k in range(1, slabs):
         row_copies[k - 1].wait_recv()
@@ -455,21 +480,28 @@
     )
 
     def apply(turn, field, scalar):
-        moving = send_face(turn, field)
+        moving = [send_face(turn, field, c) for c in range(2)]
         hold_field(field[...])
+        part[turn, :, 0:every] = correlate(slice(0, every))
         part[turn, :, every:] = jnp.where(lane == atoms, scalar, correlate(ends))
-        hand_on(turn, moving, 0)
-        part[turn, :, 0 : every // 2] = correlate(slice(0, every // 2))
-        hand_on(turn, moving, 1)
-        part[turn, :, every // 2 : every] = correlate(slice(every // 2, every))
         copies = start_sum(turn)
-        hand_on(turn, moving, 2)
-        plane_image(field, range(0, HALO // 2))
-        hand_on(turn, moving, 3)
-        plane_image(field, range(HALO // 2, HALO))
-        shared = share_sum(turn, copies)
+        face = list(moving)
+        handed = []
         for c in range(CHUNKS):
-            across_planes(turn, field, moving, c)
+            if c + 2 < CHUNKS:
+                face.append(send_face(turn, field, c + 2))
+            face[c].wait_recv()
+            handed.append(hand_over(turn, c))
+            if c < 3:
+                plane_image(field, range(2 * c, 2 * c + 2))
+            if c == SUM_AT:
+                shared = share_sum(turn, copies)
+            if c >= 4:
+                handed[c - 4].wait_recv()
+                across_planes(turn, field, c - 4)
+        for c in range(CHUNKS - 4, CHUNKS):
+            handed[c].wait_recv()
+            across_planes(turn, field, c)
         finish_sum(shared)
         last = totals[turn, :, every:]
         coefficients = jnp.concatenate(
@@ -531,13 +563,11 @@
         copy.wait_send()
 
 
-def fused(atoms, occupied, start_guess, potential, perturbation, energy, fields, in_plane):
+def fused(atoms, occupied, start_guess, potential, perturbation, energy, fields):
     slabs = lax.axis_size("dom")
     bands, cells = occupied.shape
     every = 4 * bands
     rows = every + 128
-    plane_high = in_plane.astype(jnp.bfloat16)
-    plane_low = (in_plane - plane_high.astype(np.float32)).astype(jnp.bfloat16)
     f32, bf16 = jnp.float32, jnp.bfloat16
     vmem = pl.BlockSpec(memory_space=pltpu.VMEM)
     out = jax.ShapeDtypeStruct((1, bands, cells), f32)
@@ -546,9 +576,13 @@
     return pl.pallas_call(
         functools.partial(fused_kernel, atoms, slabs),
         out_shape=(out, out),
-        in_specs=[vmem] * 8,
+        in_specs=[pl.BlockSpec(memory_space=pl.ANY)] * 2 + [vmem] * 4,
         out_specs=(vmem, vmem),
         scratch_shapes=[
+            field,
+            field,
+            pltpu.VMEM((PLANE, PLANE), bf16),
+            pltpu.VMEM((PLANE, PLANE), bf16),
             pltpu.VMEM((3, bands, cells), f32),
             pltpu.VMEM((rows, cells), bf16),
             pltpu.VMEM((rows, cells), bf16),
@@ -580,6 +614,7 @@
             dma((slabs,)),
             dma((slabs,)),
             dma((slabs,)),
+            dma((2,)),
         ],
         compiler_params=pltpu.CompilerParams(
             collective_id=0, has_side_effects=True, vmem_limit_bytes=40 * 1024 * 1024
@@ -591,8 +626,6 @@
         perturbation,
         energy,
         fields,
-        jnp.asarray(plane_high),
-        jnp.asarray(plane_low),
     )
 
 
@@ -615,7 +648,6 @@
     fields = atom_fields(
         slabs, cells, beta_radial, beta_slope, sphere_offset, atom_owner, atom_site, displaced
     )
-    in_plane = plane_matrix()
     fits = bands == 8 * slabs and lax.axis_size("band") == 4 and atoms % 16 == 0 and atoms <= 112
     if fits and cells == HALO * PLANE:
         return fused(
@@ -626,7 +658,6 @@
             perturbation,
             band_energy[:, None],
             fields,
-            in_plane,
         )
     answer, residual = plain(
         occupied,
@@ -636,7 +667,7 @@
         band_energy[:, None],
         fields[:atoms],
         fields[atoms : atoms + 8],
-        jnp.asarray(in_plane),
+        jnp.asarray(plane_matrix()),
     )
     return answer[None], residual[None]
 

time: 85.1 us -> 76.8 us (0.902)
  Pallas kernels: 78.8 us -> 72.2 us
  local copies, waits for them, and re-layouts: 4.71 us -> 2.91 us
    pallas_call x1, Pallas kernels: 77 us -> 70.5 us  [fused(): pl.pallas_call(functools.partial(fused_kernel, atoms, slabs), out_shape=(...]
    unnamed x26 -> x22, local copies, waits for them, and re-layouts: 4.61 us -> 2.81 us
where the time goes in v3:
time: 76.8 us; the launch traced here: 76.5 us
  Pallas kernels  72.2 us (94%)
  local copies, waits for them, and re-layouts  2.91 us (4%)
  between operations  1.35 us (2%)
    pallas_call x1, Pallas kernels, fused(): pl.pallas_call(functools.partial(fused_kernel, atoms, slabs), out_shape=(...  70.5 us
    unnamed x22, local copies, waits for them, and re-layouts  2.81 us
    pallas_call x1, Pallas kernels, atom_fields(): pl.pallas_call(functools.partial(fields_kernel, slabs, depth), out_shape=...  1.75 us

profile of v3, /device:TPU:0, one launch (start us, length us, event | category | flops | bytes accessed | tf_op | source)
XLA Modules:
  0.0 76.5 jit_solution(11104544982116279745)
XLA Ops:
  0.6 0.0 copy-start.8
  1.3 0.0 copy-done.8
  1.3 0.0 copy-start.9
  1.3 0.6 copy-done.9
  2.0 0.0 copy-start.2
  2.0 0.0 copy-start.4
  2.0 0.0 copy-start.5
  2.0 0.0 copy-start.6
  2.0 0.0 copy-start.7
  2.0 0.1 copy.13.energy
  2.1 0.6 copy-done.2
  2.7 0.0 copy-done.4
  2.7 0.0 copy-done.5
  2.7 0.0 copy-done.6
  2.7 0.0 copy-done.7
  2.7 0.0 copy-start
  2.7 0.0 copy-start.1
  2.7 0.0 copy-start.3
  2.7 1.7 %shard_map.122.fields = f32[128,1536]{1,0:T(8,128)S(1)} custom-call(f32[1,512]{1,0:T(1,128)S(1)} %bitcast.5, f32[1,512]{1,0:T(1,128)S(1)} %bitcast.6, s32[3,512]{1,0:T(4,128)S(1)} %copy-done.2, s32[32]{0:T(128)S(1)} %copy-done.7, s32[3,32]{1,0:T(4,128)S(1)} %copy-done.6, s32[1]{0:T(128)S(6)} %copy.16.displaced), custom_call_target="tpu_custom_call" | custom-call | tf_op jit(solution)/shard_map/pallas_call | solution.py:92
  4.5 0.0 copy-done
  4.5 0.0 copy-done.1
  4.5 0.0 copy-done.3
  4.5 70.5 %shard_map.123 = (f32[1,64,1536]{2,1,0:T(8,128)S(1)}, f32[1,64,1536]{2,1,0:T(8,128)S(1)}) custom-call(f32[64,1536]{1,0:T(8,128)S(1)} %copy-done, f32[64,1536]{1,0:T(8,128)S(1)} %bitcast.4, f32[1,1536]{1,0:T(1,128)S(1)} %broadcast_in_dim.12.pot, f32[1,1536]{1,0:T(1,128)S(1)} %copy-done.3, f32[64,1]{1,0:T(8,128)S(1)} %copy.13.energy, ...), custom_call_target="tpu_custom_call" | custom-call | tf_op jit(solution)/shard_map/pallas_call | solution.py:576
  75.0 0.7 copy.17
  75.8 0.7 copy.18
  (1 shorter events, 0.0 us)
Async XLA Ops:
  0.6 0.7 copy-start.8
  1.3 0.7 copy-start.9
  2.0 0.7 copy-start.2
  2.0 0.7 copy-start.4
  2.0 0.7 copy-start.5
  2.0 0.7 copy-start.6
  2.0 0.7 copy-start.7
  2.7 1.8 %copy-start = (f32[64,1536]{1,0:T(8,128)S(1)}, f32[64,1536]{1,0:T(8,128)}, u32[]{:S(2)}) copy-start(f32[64,1536]{1,0:T(8,128)} %occ_in.1) | copy-start | bytes 1179652
  2.7 1.8 %copy-start.1 = (f32[1,64,1536]{2,1,0:T(8,128)S(1)}, f32[1,64,1536]{2,1,0:T(8,128)}, u32[]{:S(2)}) copy-start(f32[1,64,1536]{2,1,0:T(8,128)} %param.12) | copy-start | bytes 1179652
  2.7 1.8 %copy-start.3 = (f32[1,1536]{1,0:T(1,128)S(1)}, f32[1,1536]{1,0:T(1,128)}, u32[]{:S(2)}) copy-start(f32[1,1536]{1,0:T(1,128)} %pert.1) | copy-start | bytes 18436

commit v4 on v3

--- a/solution.py
+++ b/solution.py
@@ -499,9 +499,6 @@
             if c >= 4:
                 handed[c - 4].wait_recv()
                 across_planes(turn, field, c - 4)
-        for c in range(CHUNKS - 4, CHUNKS):
-            handed[c].wait_recv()
-            across_planes(turn, field, c)
         finish_sum(shared)
         last = totals[turn, :, every:]
         coefficients = jnp.concatenate(
@@ -512,6 +509,9 @@
             axis=1,
         )
         image[...] += back(coefficients)
+        for c in range(CHUNKS - 4, CHUNKS):
+            handed[c].wait_recv()
+            across_planes(turn, field, c)
         return last[:, atoms : atoms + 1]
 
     def dot(u, v):

time: 76.8 us -> 76.5 us (level)
  no operation moved by 1% of the time
where the time goes in v4:
time: 76.5 us; the launch traced here: 76.3 us
  Pallas kernels  72 us (94%)
  local copies, waits for them, and re-layouts  2.91 us (4%)
  between operations  1.35 us (2%)
    pallas_call x1, Pallas kernels, fused(): pl.pallas_call(functools.partial(fused_kernel, atoms, slabs), out_shape=(...  70.2 us
    unnamed x22, local copies, waits for them, and re-layouts  2.81 us
    pallas_call x1, Pallas kernels, atom_fields(): pl.pallas_call(functools.partial(fields_kernel, slabs, depth), out_shape=...  1.75 us

profile of v4, /device:TPU:0, one launch (start us, length us, event | category | flops | bytes accessed | tf_op | source)
XLA Modules:
  0.0 76.3 jit_solution(11207360278248796868)
XLA Ops:
  0.6 0.0 copy-start.8
  1.3 0.0 copy-done.8
  1.3 0.0 copy-start.9
  1.3 0.6 copy-done.9
  2.0 0.0 copy-start.2
  2.0 0.0 copy-start.4
  2.0 0.0 copy-start.5
  2.0 0.0 copy-start.6
  2.0 0.0 copy-start.7
  2.0 0.1 copy.13.energy
  2.1 0.6 copy-done.2
  2.7 0.0 copy-done.4
  2.7 0.0 copy-done.5
  2.7 0.0 copy-done.6
  2.7 0.0 copy-done.7
  2.7 0.0 copy-start
  2.7 0.0 copy-start.1
  2.7 0.0 copy-start.3
  2.7 1.7 %shard_map.122.fields = f32[128,1536]{1,0:T(8,128)S(1)} custom-call(f32[1,512]{1,0:T(1,128)S(1)} %bitcast.5, f32[1,512]{1,0:T(1,128)S(1)} %bitcast.6, s32[3,512]{1,0:T(4,128)S(1)} %copy-done.2, s32[32]{0:T(128)S(1)} %copy-done.7, s32[3,32]{1,0:T(4,128)S(1)} %copy-done.6, s32[1]{0:T(128)S(6)} %copy.16.displaced), custom_call_target="tpu_custom_call" | custom-call | tf_op jit(solution)/shard_map/pallas_call | solution.py:92
  4.5 0.0 copy-done
  4.5 0.0 copy-done.1
  4.5 0.0 copy-done.3
  4.5 70.2 %shard_map.123 = (f32[1,64,1536]{2,1,0:T(8,128)S(1)}, f32[1,64,1536]{2,1,0:T(8,128)S(1)}) custom-call(f32[64,1536]{1,0:T(8,128)S(1)} %copy-done, f32[64,1536]{1,0:T(8,128)S(1)} %bitcast.4, f32[1,1536]{1,0:T(1,128)S(1)} %broadcast_in_dim.12.pot, f32[1,1536]{1,0:T(1,128)S(1)} %copy-done.3, f32[64,1]{1,0:T(8,128)S(1)} %copy.13.energy, ...), custom_call_target="tpu_custom_call" | custom-call | tf_op jit(solution)/shard_map/pallas_call | solution.py:576
  74.8 0.7 copy.17
  75.5 0.7 copy.18
  (1 shorter events, 0.0 us)
Async XLA Ops:
  0.6 0.7 copy-start.8
  1.3 0.7 copy-start.9
  2.0 0.7 copy-start.2
  2.0 0.7 copy-start.4
  2.0 0.7 copy-start.5
  2.0 0.7 copy-start.6
  2.0 0.7 copy-start.7
  2.7 1.8 %copy-start = (f32[64,1536]{1,0:T(8,128)S(1)}, f32[64,1536]{1,0:T(8,128)}, u32[]{:S(2)}) copy-start(f32[64,1536]{1,0:T(8,128)} %occ_in.1) | copy-start | bytes 1179652
  2.7 1.8 %copy-start.1 = (f32[1,64,1536]{2,1,0:T(8,128)S(1)}, f32[1,64,1536]{2,1,0:T(8,128)}, u32[]{:S(2)}) copy-start(f32[1,64,1536]{2,1,0:T(8,128)} %param.12) | copy-start | bytes 1179652
  2.7 1.8 %copy-start.3 = (f32[1,1536]{1,0:T(1,128)S(1)}, f32[1,1536]{1,0:T(1,128)}, u32[]{:S(2)}) copy-start(f32[1,1536]{1,0:T(1,128)} %pert.1) | copy-start | bytes 18436
